TPU v7x, 32 devices: a whole 2x2x4 slice. The times are simulated.
32 devices in a mesh: order: 8 (over y, x, core), chan: 4 (over z).
Axes of the slice: x: 2, y: 2, z: 4, core: 2. Of those that a mesh axis runs over, the one named last changes fastest.
Arguments:
- fields: bfloat16 [32, 3, 720, 2, 2, 256], P('order', None, None, None, None, 'chan'), may hold values from -6 to 6
- wigner: bfloat16 [32, 3, 721, 720], P('order'), may hold values from -0.21875 to 0.21875
- mix_weight: bfloat16 [736, 3, 256, 256], P('order', None, 'chan'), may hold values from -0.375 to 0.375
- pair_orders: int32 [32], P('order'), may hold values from 0 to 359, as said below
- deg_counts: int32 [8], replicated, may hold values from 1 to 92, 720 in all
Outputs:
- out_fields: bfloat16 [32, 3, 720, 2, 2, 256], P('order', None, None, None, None, 'chan')
Inputs may be any that keep to these rules, and one draw needn't show every extreme that they name: Distinct lower orders; pair i holds orders m = pair_orders[i] and 719 - m, and pair i lies on order device i // 4. Owner e holds the next deg_counts[e] degrees after those of owners before it, in slots e * 92 onward, one slot each; the counts sum to 720, and slots past an owner's count are not read.
All inputs are finite; a program needn't handle non-finite values.
Results may differ from a plain program's by a relative error of at most 0.012.
Values may be sent and summed in bfloat16 or wider, within the bound.
A program may use at most 256 MiB of HBM per device.

v0:
```python
import jax
import jax.numpy as jnp
from jax import lax
from jax.sharding import PartitionSpec as P


def slot_for(degree, ends_at, slot_count):
    above = (degree[..., None] >= ends_at).astype(jnp.int32)
    owner_of = jnp.sum(above, axis=-1)
    start_of = jnp.max(jnp.where(above > 0, ends_at, 0), axis=-1)
    return owner_of * slot_count + degree - start_of


def take_rows(source_rows, row_picks):
    return jax.vmap(lambda row_block, pick_block: jnp.take(row_block, pick_block, axis=1))(
        source_rows, row_picks
    )


def per_device(fields, wigner, mix_weight, pair_orders, deg_counts):
    pair_count = fields.shape[0]
    spin_count = fields.shape[1]
    cycle_count = fields.shape[2]
    chan_width = fields.shape[5]
    row_width = 2 * chan_width
    degree_total = wigner.shape[2] - 1
    upper_start = degree_total // 2 + 1
    upper_rows = degree_total + 1 - upper_start
    owners = lax.axis_size("order")
    slot_count = mix_weight.shape[0]
    ends_at = jnp.cumsum(deg_counts)
    starts_at = ends_at - deg_counts
    stacked = fields.reshape(pair_count, spin_count, cycle_count, 2, row_width)
    lower_rows = jnp.einsum(
        "psrj,psjn->psrn",
        wigner[:, :, :degree_total],
        stacked[:, :, :, 0],
        preferred_element_type=jnp.float32,
    ).astype(jnp.bfloat16)
    higher_rows = jnp.einsum(
        "psrj,psjn->psrn",
        wigner[:, :, upper_start:],
        stacked[:, :, :, 1],
        preferred_element_type=jnp.float32,
    ).astype(jnp.bfloat16)
    zero_row = jnp.zeros((pair_count, spin_count, 1, row_width), jnp.bfloat16)
    lower_rows = jnp.concatenate([lower_rows, zero_row], axis=2)
    higher_rows = jnp.concatenate([higher_rows, zero_row], axis=2)
    low_order = pair_orders[:, None, None]
    high_order = degree_total - 1 - low_order
    slot_iota = jnp.arange(slot_count, dtype=jnp.int32)
    wanted = (starts_at[:, None] + slot_iota[None, :])[None]
    live_slot = (slot_iota[None, :] < deg_counts[:, None])[None]
    lower_pick = jnp.where(live_slot & (wanted >= low_order), wanted - low_order, degree_total)
    higher_pick = jnp.where(
        live_slot & (wanted >= high_order), wanted + 1 - upper_start, upper_rows
    )
    outgoing = jnp.stack(
        [take_rows(lower_rows, lower_pick), take_rows(higher_rows, higher_pick)], axis=1
    )
    outgoing = outgoing.transpose(3, 4, 2, 0, 1, 5)
    received = lax.all_to_all(outgoing, "order", split_axis=0, concat_axis=0, tiled=True)
    item_count = received.shape[3]
    split_rows = received.reshape(owners, slot_count, spin_count, item_count, 2, 2, chan_width)
    partials = jnp.einsum(
        "nksqorc,kscd->nksqord", split_rows, mix_weight, preferred_element_type=jnp.float32
    )
    mixed_rows = lax.psum_scatter(
        partials.astype(jnp.bfloat16), "chan", scatter_dimension=6, tiled=True
    )
    mixed_rows = mixed_rows.reshape(owners, slot_count, spin_count, item_count, 2, row_width)
    returned = lax.all_to_all(mixed_rows, "order", split_axis=0, concat_axis=0, tiled=True)
    empty_slot = owners * slot_count
    returned_rows = returned.reshape(empty_slot, spin_count, pair_count, 2, row_width)
    returned_rows = jnp.concatenate(
        [returned_rows, jnp.zeros((1, spin_count, pair_count, 2, row_width), jnp.bfloat16)], axis=0
    )
    returned_rows = returned_rows.transpose(2, 3, 1, 0, 4)
    lower_degree = pair_orders[:, None] + jnp.arange(degree_total, dtype=jnp.int32)[None, :]
    lower_back = jnp.where(
        lower_degree < degree_total,
        slot_for(jnp.minimum(lower_degree, degree_total - 1), ends_at, slot_count),
        empty_slot,
    )
    higher_degree = jnp.arange(upper_rows, dtype=jnp.int32) + (upper_start - 1)
    higher_back = jnp.where(
        higher_degree[None, :] >= high_order[:, :, 0],
        slot_for(higher_degree, ends_at, slot_count)[None, :],
        empty_slot,
    )
    lower_inputs = take_rows(returned_rows[:, 0], lower_back)
    higher_inputs = take_rows(returned_rows[:, 1], higher_back)
    lower_field = jnp.einsum(
        "psrj,psrn->psjn",
        wigner[:, :, :degree_total],
        lower_inputs,
        preferred_element_type=jnp.float32,
    )
    higher_field = jnp.einsum(
        "psrj,psrn->psjn",
        wigner[:, :, upper_start:],
        higher_inputs,
        preferred_element_type=jnp.float32,
    )
    combined = jnp.stack([lower_field, higher_field], axis=3)
    return combined.reshape(pair_count, spin_count, cycle_count, 2, 2, chan_width).astype(
        jnp.bfloat16
    )


def solution(mesh):
    in_specs = (
        P("order", None, None, None, None, "chan"),
        P("order", None, None, None),
        P("order", None, "chan", None),
        P("order"),
        P(),
    )
    out_specs = P("order", None, None, None, None, "chan")
    return jax.shard_map(
        per_device, mesh=mesh, in_specs=in_specs, out_specs=out_specs, check_vma=False
    )
```

profile of v0, /device:TPU:16, one launch (start us, length us, event | category | flops | bytes accessed | tf_op | source)
XLA Modules:
  0.0 801.5 jit_solution(16235901955490344673)
XLA Ops:
  6.5 9.1 %fusion.16 = bf16[4,3,720,128]{3,2,1,0:T(8,128)(2,1)} fusion(bf16[4,3,720,2,128]{2,4,3,1,0:T(8,128)(2,1)} %bitcast.93, bf16[4,3,721,720]{2,3,1,0:T(8,128)(2,1)} %param.6), kind=kOutput, calls=%fused_computation.27 | convolution fusion | flops 1593630720 | bytes 17842176 | tf_op jit(solution)/shard_map/psrj,psjn->psrn/dot_general | solution.py:34
  15.6 0.9 copy-done.1
  16.6 8.4 %fusion.19 = bf16[4,3,360,128]{3,2,1,0:T(8,128)(2,1)} fusion(bf16[4,3,720,2,128]{2,4,3,1,0:T(8,128)(2,1)} %bitcast.94, bf16[4,3,721,720]{2,3,1,0:T(8,128)(2,1)S(1)} %copy-done.1), kind=kOutput, calls=%fused_computation.28 | convolution fusion | flops 796815360 | bytes 10100736 | tf_op jit(solution)/shard_map/psrj,psjn->psrn/dot_general | solution.py:40
  25.0 0.2 reduce-window.8
  25.3 0.1 fusion.25
  25.4 0.1 fusion.33
  25.5 0.1 reshape.387
  25.6 2.8 copy.130
  28.4 0.1 reshape.393
  28.5 1.8 copy.131
  30.3 2.7 concatenate.11.clone
  33.0 0.6 concatenate.12.clone
  33.6 28.4 %gather_fusion = bf16[2944,3,128]{2,1,0:T(4,128)(2,1)} fusion(bf16[4,3,721,128]{3,1,2,0:T(4,128)(2,1)} %concatenate.11.clone, s32[2944]{0:T(1024)S(1)} %reshape.387), kind=kCustom, calls=%fused_computation | custom fusion | bytes 4545536 | tf_op jit(solution)/shard_map/vmap(jit(_take))/gather | solution.py:15
  62.0 18.4 %gather_fusion.1 = bf16[2944,3,128]{2,1,0:T(4,128)(2,1)} fusion(bf16[4,3,361,128]{3,1,2,0:T(4,128)(2,1)S(1)} %concatenate.12.clone, s32[2944]{0:T(1024)S(1)} %reshape.393), kind=kCustom, calls=%fused_computation.1 | custom fusion | bytes 4545536 | tf_op jit(solution)/shard_map/vmap(jit(_take))/gather | solution.py:15
  80.4 4.4 bitcast_select_fusion
  84.7 0.4 maximum_bitcast_fusion
  85.2 3.5 copy.96
  88.7 56.2 %all_to_all.10 = bf16[8,92,3,4,2,128]{5,3,4,2,1,0:T(4,128)(2,1)} all-to-all(bf16[8,92,3,4,2,128]{5,3,4,2,1,0:T(4,128)(2,1)S(1)} %copy.96), channel_id=1, replica_groups=mesh['order'=8,'chan'=4] {'order'}, dimensions={0} | all-to-all | bytes 9043968 | tf_op jit(solution)/shard_map/all_to_all | solution.py:62
  144.9 10.1 %copy.97 = bf16[8,92,3,4,2,128]{1,5,4,3,2,0:T(8,128)(2,1)} copy(bf16[8,92,3,4,2,128]{5,3,4,2,1,0:T(4,128)(2,1)} %all_to_all.10) | data formatting | bytes 9043968 | tf_op jit(solution)/shard_map/all_to_all | solution.py:62
  154.9 16.4 %copy.98 = bf16[8,92,3,4,2,2,64]{6,0,5,4,3,2,1:T(8,128)(2,1)} copy(bf16[8,92,3,4,2,2,64]{1,6,5,4,3,2,0:T(8,128)(2,1)} %bitcast.84) | data formatting | bytes 9043968 | tf_op jit(solution)/shard_map/reshape | solution.py:64
  171.3 15.8 %convert_bitcast_fusion = bf16[8,92,3,4,2,2,256]{6,0,5,4,3,2,1:T(8,128)(2,1)} fusion(bf16[8,92,3,4,2,2,64]{6,0,5,4,3,2,1:T(8,128)(2,1)} %copy.98, bf16[92,3,64,256]{3,2,1,0:T(8,128)(2,1)} %param.7), kind=kOutput, calls=%fused_computation.4 | convolution fusion | flops 1166671872 | bytes 31653888 | tf_op jit(solution)/shard_map/nksqorc,kscd->nksqord/dot_general | solution.py:65
  187.1 31.6 %copy.99 = bf16[8,92,3,4,2,2,256]{1,0,5,4,3,2,6:T(8,128)(2,1)} copy(bf16[8,92,3,4,2,2,256]{6,0,5,4,3,2,1:T(8,128)(2,1)} %convert_bitcast_fusion) | data formatting | bytes 36175872 | tf_op jit(solution)/shard_map/convert_element_type | solution.py:69
  218.7 415.5 %reduce-scatter.2.cloned.1.call-done = bf16[8,92,3,4,2,2,64]{1,0,5,4,3,2,6:T(8,128)(2,1)} async-done(((bf16[8,92,3,4,2,2,256]{1,0,5,4,3,2,6:T(8,128)(2,1)}), bf16[8,92,3,4,2,2,64]{1,0,5,4,3,2,6:T(8,128)(2,1)}) %reduce-scatter.2.cloned.1.call-update) | async-done | bytes 4522000 | tf_op jit(solution)/shard_map/reduce_scatter | solution.py:68
  634.3 9.5 %copy.100 = bf16[8,92,3,4,2,2,64]{1,6,5,4,3,2,0:T(8,128)(2,1)} copy(bf16[8,92,3,4,2,2,64]{1,0,5,4,3,2,6:T(8,128)(2,1)} %reduce-scatter.2.cloned.1.call-done) | data formatting | bytes 9043968 | tf_op jit(solution)/shard_map/reduce_scatter | solution.py:68
  643.8 10.2 %copy.101 = bf16[8,92,3,4,2,128]{5,3,4,2,1,0:T(4,128)(2,1)} copy(bf16[8,92,3,4,2,128]{1,5,4,3,2,0:T(8,128)(2,1)} %bitcast.83) | data formatting | bytes 9043968 | tf_op jit(solution)/shard_map/reshape | solution.py:71
  654.0 4.8 all-to-all-start.1
  658.8 0.2 convert_reduce_fusion
  659.0 0.1 fusion.37
  659.1 0.1 reshape.399
  659.2 0.1 convert_reduce_fusion.1
  659.3 0.1 reshape.405
  659.5 0.1 compare_and_fusion
  659.6 51.8 %all-to-all-done.1 = bf16[8,92,3,4,2,128]{5,3,4,2,1,0:T(4,128)(2,1)} async-done(((bf16[8,92,3,4,2,128]{5,3,4,2,1,0:T(4,128)(2,1)}), bf16[8,92,3,4,2,128]{5,3,4,2,1,0:T(4,128)(2,1)}, u32[]{:S(2)}, u32[]{:S(2)}) %all-to-all-start.1) | async-done | bytes 4522016 | tf_op jit(solution)/shard_map/all_to_all | solution.py:72
  711.4 3.0 copy.121
  714.5 0.3 pad_bitcast_fusion
  714.8 1.7 slice_bitcast_fusion.5
  716.5 1.6 copy.104
  718.0 25.2 %gather_fusion.2 = bf16[2880,3,128]{2,1,0:T(4,128)(2,1)} fusion(bf16[4,3,737,128]{3,1,2,0:T(4,128)(2,1)S(1)} %copy.104, s32[2880]{0:T(1024)S(1)} %reshape.399), kind=kCustom, calls=%fused_computation.2 | custom fusion | bytes 4446720 | tf_op jit(solution)/shard_map/vmap(jit(_take))/gather | solution.py:15
  743.2 2.2 copy.105
  745.4 7.8 convert_bitcast_fusion.2
  753.2 3.2 copy.108
  756.5 4.8 copy.110
  761.3 14.7 %gather_fusion.3 = bf16[1440,3,128]{2,1,0:T(4,128)(2,1)} fusion(bf16[4,3,737,128]{3,1,2,0:T(4,128)(2,1)} %copy.110, s32[1440]{0:T(1024)S(1)} %reshape.405), kind=kCustom, calls=%fused_computation.3 | custom fusion | bytes 2223360 | tf_op jit(solution)/shard_map/vmap(jit(_take))/gather | solution.py:15
  776.0 1.5 copy.111
  777.6 7.9 convert_bitcast_fusion.1
  785.4 4.2 copy.114
  789.6 2.1 pad_maximum_fusion
  791.8 2.7 copy.115
  (16 shorter events, 0.4 us)
Async XLA Ops:
  6.5 627.8 %reduce-scatter.2.cloned.1.call-start = ((), (), s32[]{:S(2)}) async-start(), calls=%async_computation.3 | async-start | bytes 31457280 | tf_op jit(solution)/shard_map/reduce_scatter | solution.py:68
  6.5 10.0 %copy-start.1 = (bf16[4,3,721,720]{2,3,1,0:T(8,128)(2,1)S(1)}, bf16[4,3,721,720]{2,3,1,0:T(8,128)(2,1)}, u32[]{:S(2)}) copy-start(bf16[4,3,721,720]{2,3,1,0:T(8,128)(2,1)} %param.6) | copy-start | bytes 37376644
  16.6 8.4 %copy-start.2 = (s32[8]{0:T(128)S(1)}, s32[8]{0:T(128)}, u32[]{:S(2)}) copy-start(s32[8]{0:T(128)} %param.9) | copy-start | bytes 100
  16.6 8.7 %copy-start = (s32[4]{0:T(128)S(1)}, s32[4]{0:T(128)}, u32[]{:S(2)}) copy-start(s32[4]{0:T(128)} %param.8) | copy-start | bytes 52
  654.0 57.4 %all-to-all-start.1 = ((bf16[8,92,3,4,2,128]{5,3,4,2,1,0:T(4,128)(2,1)}), bf16[8,92,3,4,2,128]{5,3,4,2,1,0:T(4,128)(2,1)}, u32[]{:S(2)}, u32[]{:S(2)}) async-start(bf16[8,92,3,4,2,128]{5,3,4,2,1,0:T(4,128)(2,1)} %copy.101), calls=%async_computation.2 | async-start | bytes 9043968 | tf_op jit(solution)/shard_map/all_to_all | solution.py:72
Sparse Core Ops, SparseCore 0:
  218.9 415.3 reduce-scatter.1
where the time goes:
time: 812 us; the launch traced here: 802 us
  waiting for transfers between devices  467 us (58%)
  local copies, waits for them, and re-layouts  202 us (25%)
  blocking collectives  56.2 us (7%)
  matrix products  49 us (6%)
  between operations  13.7 us (2%)
    reduce_scatter x1, waiting for transfers between devices, per_device(): lax.psum_scatter(partials.astype(jnp.bfloat16), 'chan', scatter_dimension...  416 us
    gather x10, local copies, waits for them, and re-layouts, take_rows(): jnp.take(row_block, pick_block, axis=1)  90.7 us
    all_to_all x1, blocking collectives, per_device(): lax.all_to_all(outgoing, 'order', split_axis=0, concat_axis=0, tiled=True)  56.2 us
    all_to_all x1, waiting for transfers between devices, per_device(): lax.all_to_all(mixed_rows, 'order', split_axis=0, concat_axis=0, tiled=True)  51.8 us
    convert_element_type x1, local copies, waits for them, and re-layouts, per_device(): partials.astype(jnp.bfloat16)  31.6 us
    reshape x1, local copies, waits for them, and re-layouts, per_device(): received.reshape(owners, slot_count, spin_count, item_count, 2, 2, chan_w...  16.4 us
  transfers between devices with their start and end apart: 2, of which 2 were waited for; matrix products, arithmetic and copies ran while one was open for 0% of the time, Pallas kernels for 0%

commit v1 on v0

v1 whole, which is shorter than its diff:
```python
import functools
import jax
import jax.numpy as jnp
from jax import lax
from jax.experimental import pallas as pl
from jax.experimental.pallas import tpu as pltpu
from jax.sharding import PartitionSpec as P

F32, BF16 = jnp.float32, jnp.bfloat16
FIRST = (((0,), (0,)), ((), ()))
LAST = (((1,), (1,)), ((), ()))
PARAMS = pltpu.CompilerParams(vmem_limit_bytes=48 * 1024 * 1024)


def analyse_kernel(order_ref, degree_ref, table_ref, field_ref, out_ref, low_pick, high_pick):
    pair = pl.program_id(0)
    rows = table_ref.shape[3]
    half = field_ref.shape[2] // 2

    @pl.when(pl.program_id(1) == 0)
    def _():
        low = order_ref[pair]
        degree = degree_ref[...]
        at = lax.broadcasted_iota(jnp.int32, low_pick.shape, 1)
        low_pick[...] = jnp.where(at == degree - low, 1.0, 0.0).astype(BF16)
        high = jnp.where(degree >= rows - 2 - low, degree + 1, -1)
        high_pick[...] = jnp.where(at == high, 1.0, 0.0).astype(BF16)

    coef = jnp.dot(field_ref[0, 0], table_ref[0, 0], preferred_element_type=F32).astype(BF16)
    low_rows = lax.dot_general(low_pick[...], coef[:half], LAST, preferred_element_type=F32)
    high_rows = lax.dot_general(high_pick[...], coef[half:], LAST, preferred_element_type=F32)
    dests, _, _, slots, _ = out_ref.shape
    out_ref[:, 0, 0, :, :half] = low_rows.reshape(dests, slots, half).astype(BF16)
    out_ref[:, 0, 0, :, half:] = high_rows.reshape(dests, slots, half).astype(BF16)


def synthesise_kernel(order_ref, degree_ref, table_ref, mixed_ref, out_ref, low_pick, high_pick):
    pair = pl.program_id(0)
    rows = table_ref.shape[3]
    half = mixed_ref.shape[4] // 2

    @pl.when(pl.program_id(1) == 0)
    def _():
        low = order_ref[pair]
        degree = degree_ref[...]
        at = lax.broadcasted_iota(jnp.int32, low_pick.shape, 1)
        low_pick[...] = jnp.where(at == degree - low, 1.0, 0.0).astype(BF16)
        high = jnp.where(degree >= rows - 2 - low, degree + 1, -1)
        high_pick[...] = jnp.where(at == high, 1.0, 0.0).astype(BF16)

    dests, _, _, slots, width = mixed_ref.shape
    mixed = mixed_ref[:, 0, 0].astype(F32).reshape(dests * slots, width).astype(BF16)
    low_rows = lax.dot_general(mixed[:, :half], low_pick[...], FIRST, preferred_element_type=F32)
    high_rows = lax.dot_general(mixed[:, half:], high_pick[...], FIRST, preferred_element_type=F32)
    back = jnp.concatenate([low_rows, high_rows], axis=0).astype(BF16)
    out_ref[0, 0] = lax.dot_general(
        back, table_ref[0, 0], LAST, preferred_element_type=F32
    ).astype(BF16)


def mix_kernel(slot_count, where_ref, x_ref, *refs):
    weights, out_ref = refs[:-1], refs[-1]
    blocks = len(weights)
    _, spins, _, items, width = x_ref.shape
    chans = weights[0].shape[2]
    parts = width // chans
    me = where_ref[0]
    live = pl.program_id(0) < slot_count

    @pl.when(live)
    def _():
        for s in range(spins):
            held = []
            for shift in range(blocks):
                x = x_ref[0, s, lax.rem(me - shift + blocks, blocks)]
                held.append(
                    jnp.concatenate([x[:, i * chans:(i + 1) * chans] for i in range(parts)], axis=0)
                )
            w = jnp.concatenate([weight[0, s] for weight in weights], axis=0)
            y = jnp.dot(jnp.concatenate(held, axis=1), w, preferred_element_type=F32).astype(BF16)
            for g in range(blocks):
                out_ref[0, s, g] = jnp.concatenate(
                    [y[i * items:(i + 1) * items, g * chans:(g + 1) * chans] for i in range(parts)],
                    axis=1,
                )

    @pl.when(jnp.logical_not(live))
    def _():
        out_ref[...] = jnp.zeros_like(out_ref)


def per_device(fields, wigner, mix_weight, pair_orders, deg_counts):
    pairs, spins, cycles, _, _, chans = fields.shape
    rows = wigner.shape[2]
    width = 4 * chans
    owners, blocks = lax.axis_size("order"), lax.axis_size("chan")
    slots = mix_weight.shape[0] // blocks
    padded = -(-slots // 8) * 8
    dests = owners * blocks
    me = lax.axis_index("chan")

    starts = jnp.cumsum(deg_counts) - deg_counts
    within = jnp.arange(padded, dtype=jnp.int32)
    slot = jnp.arange(blocks, dtype=jnp.int32)[:, None] * slots + within[None, :]
    real = (within[None, None, :] < slots) & (slot[None] < deg_counts[:, None, None])
    degree = jnp.where(real, starts[:, None, None] + slot[None], -(1 << 20)).reshape(-1, 1)
    total = dests * padded

    sent = []
    for shift in range(1, blocks):
        to = lax.rem(me + shift, blocks)
        sent.append(lax.dynamic_slice_in_dim(mix_weight, to * slots, slots, axis=0))
    degree, *sent = lax.optimization_barrier((degree, *sent))
    weights = [mix_weight]
    for shift in range(1, blocks):
        ring = [(g, (g + shift) % blocks) for g in range(blocks)]
        weights.append(lax.ppermute(sent[shift - 1], "chan", ring))
    table = wigner.transpose(0, 1, 3, 2)
    lines = fields.transpose(0, 1, 3, 4, 5, 2).reshape(pairs, spins, width, cycles)

    table_spec = pl.BlockSpec((1, 1, cycles, rows), lambda p, s, o: (p, s, 0, 0))
    field_spec = pl.BlockSpec((1, 1, width, cycles), lambda p, s, o: (p, s, 0, 0))
    moved_spec = pl.BlockSpec((dests, 1, 1, padded, width), lambda p, s, o: (0, p, s, 0, 0))
    moved = jax.ShapeDtypeStruct((dests, pairs, spins, padded, width), BF16)
    table_flops = 4 * pairs * spins * rows * cycles * width
    cost = pl.CostEstimate(flops=table_flops, bytes_accessed=2 * wigner.size * 2, transcendentals=0)

    outgoing = pl.pallas_call(
        analyse_kernel,
        out_shape=moved,
        grid_spec=pltpu.PrefetchScalarGridSpec(
            num_scalar_prefetch=1,
            grid=(pairs, spins),
            in_specs=[pl.BlockSpec((total, 1), lambda p, s, o: (0, 0)), table_spec, field_spec],
            out_specs=moved_spec,
            scratch_shapes=[pltpu.VMEM((total, rows), BF16)] * 2,
        ),
        compiler_params=PARAMS,
        cost_estimate=cost,
        name="analyse",
    )(pair_orders, degree, table, lines)

    received = lax.all_to_all(outgoing, ("order", "chan"), split_axis=0, concat_axis=0, tiled=True)
    received = received.reshape(owners, blocks, pairs, spins, padded, width)
    items = owners * pairs
    x = received.transpose(4, 3, 1, 0, 2, 5).reshape(padded, spins, blocks, items, width)

    def block_at(k):
        return jnp.minimum(k, slots - 1)

    weight_block = (1, spins, chans, mix_weight.shape[3])
    weight_specs = [pl.BlockSpec(weight_block, lambda k, w: (w[0] * slots + block_at(k), 0, 0, 0))]
    weight_specs += [pl.BlockSpec(weight_block, lambda k, w: (block_at(k), 0, 0, 0))] * (blocks - 1)
    x_spec = pl.BlockSpec((1, spins, blocks, items, width), lambda k, w: (k, 0, 0, 0, 0))
    mixed = pl.pallas_call(
        functools.partial(mix_kernel, slots),
        out_shape=jax.ShapeDtypeStruct(x.shape, BF16),
        grid_spec=pltpu.PrefetchScalarGridSpec(
            num_scalar_prefetch=1,
            grid=(padded,),
            in_specs=[x_spec] + weight_specs,
            out_specs=x_spec,
        ),
        compiler_params=PARAMS,
        name="mix",
    )(me.reshape(1).astype(jnp.int32), x, *weights)

    mixed = mixed.reshape(padded, spins, blocks, owners, pairs, width).transpose(3, 2, 4, 1, 0, 5)
    mixed = mixed.reshape(dests, pairs, spins, padded, width)
    returned = lax.all_to_all(mixed, ("order", "chan"), split_axis=0, concat_axis=0, tiled=True)

    out = pl.pallas_call(
        synthesise_kernel,
        out_shape=jax.ShapeDtypeStruct((pairs, spins, width, cycles), BF16),
        grid_spec=pltpu.PrefetchScalarGridSpec(
            num_scalar_prefetch=1,
            grid=(pairs, spins),
            in_specs=[pl.BlockSpec((total, 1), lambda p, s, o: (0, 0)), table_spec, moved_spec],
            out_specs=field_spec,
            scratch_shapes=[pltpu.VMEM((total, rows), BF16)] * 2,
        ),
        compiler_params=PARAMS,
        cost_estimate=cost,
        name="synthesise",
    )(pair_orders, degree, table, returned)
    return out.reshape(pairs, spins, 2, 2, chans, cycles).transpose(0, 1, 5, 2, 3, 4)


def solution(mesh):
    in_specs = (
        P("order", None, None, None, None, "chan"),
        P("order", None, None, None),
        P("order", None, "chan", None),
        P("order"),
        P(),
    )
    out_specs = P("order", None, None, None, None, "chan")
    return jax.shard_map(
        per_device, mesh=mesh, in_specs=in_specs, out_specs=out_specs, check_vma=False
    )
```

time: 812 us -> 498 us (0.61)
  waiting for transfers between devices: 467 us -> 280 us
  local copies, waits for them, and re-layouts: 202 us -> 37.5 us
  Pallas kernels: 0 us -> 55.9 us
  blocking collectives: 56.2 us -> 108 us
  matrix products: 49 us -> 0 us
  between operations: 13.7 us -> 0.09 us
    reduce_scatter x1 -> x0, waiting for transfers between devices: 416 us -> none  [per_device(): lax.psum_scatter(partials.astype(jnp.bfloat16), 'chan', scatter_dimension...]
    all_to_all x1, waiting for transfers between devices: 51.8 us -> 198 us  [per_device(): lax.all_to_all(outgoing, ('order', 'chan'), split_axis=0, concat_axis=0,...]
    gather x10 -> x0, local copies, waits for them, and re-layouts: 90.7 us -> none  [take_rows(): jnp.take(row_block, pick_block, axis=1)]
    ppermute x0 -> x3, waiting for transfers between devices: none -> 81.5 us  [per_device(): weights.append(lax.ppermute(sent[shift - 1], 'chan', ring))]
    pallas_call x0 -> x3, Pallas kernels: none -> 55.9 us  [the longest x1 19.5 us: per_device(): pl.pallas_call(functools.partial(mix_kernel, slots), out_shape=jax.ShapeD...]
    all_to_all x1, blocking collectives: 56.2 us -> 108 us  [per_device(): lax.all_to_all(mixed, ('order', 'chan'), split_axis=0, concat_axis=0, til...]
    dot_general x5 -> x0, matrix products: 49 us -> none  [the longest x1 15.8 us: per_device(): jnp.einsum('nksqorc,kscd->nksqord', split_rows, mix_weight, preferred_ele...]
    convert_element_type x1 -> x0, local copies, waits for them, and re-layouts: 31.6 us -> none  [per_device(): partials.astype(jnp.bfloat16)]
  transfers between devices with their start and end apart: 2 -> 4, of which waited for: 2 -> 3; matrix products, arithmetic and copies ran while one was open for 0% -> 3% of each run, Pallas kernels for 0% -> 0%
where the time goes in v1:
time: 498 us; the launch traced here: 493 us
  waiting for transfers between devices  280 us (56%)
  blocking collectives  108 us (22%)
  Pallas kernels  55.9 us (11%)
  local copies, waits for them, and re-layouts  37.5 us (8%)
  starting transfers between devices  9.28 us (2%)
    all_to_all x1, waiting for transfers between devices, per_device(): lax.all_to_all(outgoing, ('order', 'chan'), split_axis=0, concat_axis=0,...  198 us
    all_to_all x1, blocking collectives, per_device(): lax.all_to_all(mixed, ('order', 'chan'), split_axis=0, concat_axis=0, til...  108 us
    ppermute x3, waiting for transfers between devices, per_device(): weights.append(lax.ppermute(sent[shift - 1], 'chan', ring))  81.5 us
    pallas_call x1, Pallas kernels, per_device(): pl.pallas_call(functools.partial(mix_kernel, slots), out_shape=jax.ShapeD...  19.5 us
    pallas_call x1, Pallas kernels, per_device(): pl.pallas_call(analyse_kernel, out_shape=moved, grid_spec=pltpu.PrefetchS...  18.9 us
    pallas_call x1, Pallas kernels, per_device(): pl.pallas_call(synthesise_kernel, out_shape=jax.ShapeDtypeStruct((pairs,...  17.5 us
    reshape x2, local copies, waits for them, and re-layouts, per_device(): mixed.reshape(padded, spins, blocks, owners, pairs, width)  13.9 us
  transfers between devices with their start and end apart: 4, of which 3 were waited for; matrix products, arithmetic and copies ran while one was open for 3% of the time, Pallas kernels for 0%

profile of v1, /device:TPU:16, one launch (start us, length us, event | category | flops | bytes accessed | tf_op | source)
XLA Modules:
  0.0 493.1 jit_solution(12181868507696751417)
XLA Ops:
  0.0 0.8 reduce-window.9
  0.8 0.7 bitcast_subtract_fusion
  1.5 0.1 iota_add_fusion
  1.6 0.7 add_select_fusion
  2.3 0.1 select_n.24
  2.4 0.0 copy-start.1
  2.4 6.2 %constant_dynamic-slice_fusion = (bf16[23,3,64,256]{3,2,1,0:T(8,128)(2,1)}, bf16[23,3,64,256]{3,2,1,0:T(8,128)(2,1)}, bf16[23,3,64,256]{3,2,1,0:T(8,128)(2,1)}) fusion(bf16[92,3,64,256]{3,2,1,0:T(8,128)(2,1)} %refs_0_.1, s32[]{:T(128)S(6)} %select_n.27, s32[]{:T(128)S(6)} %select_n.26, s32[]{:T(128)S(6)} %select_n.25), kind=kLoop, calls=%fused_computation.3 | loop fusion | bytes 13565964 | tf_op jit(solution)/shard_map/dynamic_slice | solution.py:112
  8.6 0.2 copy.11.degree_ref
  8.8 0.0 copy-done.1
  8.8 18.9 %analyse.1 = bf16[32,4,3,24,256]{4,3,2,1,0:T(8,128)(2,1)S(1)} custom-call(s32[4]{0:T(128)S(1)} %copy-done.1, s32[768,1]{1,0:T(8,128)S(1)} %copy.11.degree_ref, bf16[4,3,720,721]{3,2,1,0:T(8,128)(2,1)} %bitcast.23, bf16[4,3,256,720]{3,2,1,0:T(8,128)(2,1)} %bitcast.25), custom_call_target="tpu_custom_call" | custom-call | flops 6378946560 | bytes 24917760 | tf_op jit(solution)/shard_map/analyse/pallas_call | solution.py:128
  27.7 0.0 copy-start
  27.7 2.2 copy-done
  29.9 6.0 %all-to-all-start = ((bf16[32,4,3,24,256]{4,3,2,1,0:T(8,128)(2,1)}), bf16[32,4,3,24,256]{4,3,2,1,0:T(8,128)(2,1)}, u32[]{:S(2)}, u32[]{:S(2)}) async-start(bf16[32,4,3,24,256]{4,3,2,1,0:T(8,128)(2,1)} %copy-done), calls=%async_computation | async-start | bytes 9437184 | tf_op jit(solution)/shard_map/all_to_all | solution.py:143
  35.9 1.6 collective-permute-start
  37.5 0.5 collective-permute-start.1
  38.0 1.2 collective-permute-start.2
  39.2 198.1 %all-to-all-done = bf16[32,4,3,24,256]{4,3,2,1,0:T(8,128)(2,1)} async-done(((bf16[32,4,3,24,256]{4,3,2,1,0:T(8,128)(2,1)}), bf16[32,4,3,24,256]{4,3,2,1,0:T(8,128)(2,1)}, u32[]{:S(2)}, u32[]{:S(2)}) %all-to-all-start) | async-done | bytes 4718624 | tf_op jit(solution)/shard_map/all_to_all | solution.py:143
  237.4 7.3 %copy.13 = bf16[8,4,4,3,24,256]{5,2,0,1,3,4:T(4,128)(2,1)} copy(bf16[8,4,4,3,24,256]{5,4,3,2,1,0:T(8,128)(2,1)} %bitcast.6) | data formatting | bytes 9437184 | tf_op jit(solution)/shard_map/reshape | solution.py:144
  244.6 7.7 %reshape.146.x_ref = bf16[24,3,4,32,256]{4,3,2,1,0:T(8,128)(2,1)} reshape(bf16[24,3,4,8,4,256]{5,4,3,2,1,0:T(4,128)(2,1)} %bitcast.20) | data formatting | bytes 9437184 | tf_op jit(solution)/shard_map/reshape | solution.py:146
  252.3 33.8 %collective-permute-done.refs_1_ = bf16[23,3,64,256]{3,2,1,0:T(8,128)(2,1)S(1)} collective-permute-done((bf16[23,3,64,256]{3,2,1,0:T(8,128)(2,1)}, bf16[23,3,64,256]{3,2,1,0:T(8,128)(2,1)S(1)}, u32[]{:S(2)}, u32[]{:S(2)}) %collective-permute-start) | collective-permute-done | bytes 2261024 | tf_op jit(solution)/shard_map/ppermute | solution.py:117
  286.1 0.0 collective-permute-done.1.refs_2_
  286.1 47.7 %collective-permute-done.2.refs_3_ = bf16[23,3,64,256]{3,2,1,0:T(8,128)(2,1)} collective-permute-done((bf16[23,3,64,256]{3,2,1,0:T(8,128)(2,1)}, bf16[23,3,64,256]{3,2,1,0:T(8,128)(2,1)}, u32[]{:S(2)}, u32[]{:S(2)}) %collective-permute-start.2) | collective-permute-done | bytes 2261024 | tf_op jit(solution)/shard_map/ppermute | solution.py:117
  333.8 19.5 %mix.1 = bf16[24,3,4,32,256]{4,3,2,1,0:T(8,128)(2,1)} custom-call(s32[1]{0:T(128)} %bitcast.3.where_ref, bf16[24,3,4,32,256]{4,3,2,1,0:T(8,128)(2,1)} %reshape.146.x_ref, bf16[92,3,64,256]{3,2,1,0:T(8,128)(2,1)} %refs_0_.1, bf16[23,3,64,256]{3,2,1,0:T(8,128)(2,1)S(1)} %collective-permute-done.refs_1_, ...), custom_call_target="tpu_custom_call" | custom-call | tf_op jit(solution)/shard_map/mix/pallas_call | solution.py:155
  353.2 7.7 %reshape.147 = bf16[24,3,4,8,4,256]{5,4,3,2,1,0:T(4,128)(2,1)} reshape(bf16[24,3,4,32,256]{4,3,2,1,0:T(8,128)(2,1)} %mix.1) | data formatting | bytes 9437184 | tf_op jit(solution)/shard_map/reshape | solution.py:168
  360.9 6.2 %copy.10 = bf16[24,3,4,8,4,256]{5,0,1,4,2,3:T(8,128)(2,1)S(1)} copy(bf16[24,3,4,8,4,256]{5,4,3,2,1,0:T(4,128)(2,1)} %reshape.147) | data formatting | bytes 9437184 | tf_op jit(solution)/shard_map/reshape | solution.py:168
  367.1 108.4 %all_to_all.10.mixed_ref = bf16[32,4,3,24,256]{4,3,2,1,0:T(8,128)(2,1)S(1)} all-to-all(bf16[32,4,3,24,256]{4,3,2,1,0:T(8,128)(2,1)S(1)} %bitcast.21), channel_id=1, replica_groups=mesh['order'=8,'chan'=4] {'order','chan'}, dimensions={0} | all-to-all | bytes 9437184 | tf_op jit(solution)/shard_map/all_to_all | solution.py:170
  475.6 17.5 %synthesise.1 = bf16[4,3,256,720]{3,2,1,0:T(8,128)(2,1)} custom-call(s32[4]{0:T(128)S(1)} %copy-done.1, s32[768,1]{1,0:T(8,128)S(1)} %copy.11.degree_ref, bf16[4,3,720,721]{3,2,1,0:T(8,128)(2,1)} %bitcast.24, bf16[32,4,3,24,256]{4,3,2,1,0:T(8,128)(2,1)S(1)} %all_to_all.10.mixed_ref), custom_call_target="tpu_custom_call" | custom-call | flops 6378946560 | bytes 24917760 | tf_op jit(solution)/shard_map/synthesise/pallas_call | solution.py:172
  (2 shorter events, 0.0 us)
Async XLA Ops:
  2.4 6.4 %copy-start.1 = (s32[4]{0:T(128)S(1)}, s32[4]{0:T(128)}, u32[]{:S(2)}) copy-start(s32[4]{0:T(128)} %order_ref.3) | copy-start | bytes 52
  27.7 2.2 copy-start
  29.9 207.4 %all-to-all-start = ((bf16[32,4,3,24,256]{4,3,2,1,0:T(8,128)(2,1)}), bf16[32,4,3,24,256]{4,3,2,1,0:T(8,128)(2,1)}, u32[]{:S(2)}, u32[]{:S(2)}) async-start(bf16[32,4,3,24,256]{4,3,2,1,0:T(8,128)(2,1)} %copy-done), calls=%async_computation | async-start | bytes 9437184 | tf_op jit(solution)/shard_map/all_to_all | solution.py:143
  35.9 250.2 %collective-permute-start = (bf16[23,3,64,256]{3,2,1,0:T(8,128)(2,1)}, bf16[23,3,64,256]{3,2,1,0:T(8,128)(2,1)S(1)}, u32[]{:S(2)}, u32[]{:S(2)}) collective-permute-start(bf16[23,3,64,256]{3,2,1,0:T(8,128)(2,1)} %get-tuple-element.10), channel_id=1, source_target_pairs={{0,1},{1,2},{2,3},{3,0},{4,5},{5,6},{6,7},{7,4},{8,9},{9,10},{10,1... | collective-permute-start | bytes 6782984 | tf_op jit(solution)/shard_map/ppermute | solution.py:117
  37.5 248.6 %collective-permute-start.1 = (bf16[23,3,64,256]{3,2,1,0:T(8,128)(2,1)}, bf16[23,3,64,256]{3,2,1,0:T(8,128)(2,1)}, u32[]{:S(2)}, u32[]{:S(2)}) collective-permute-start(bf16[23,3,64,256]{3,2,1,0:T(8,128)(2,1)} %get-tuple-element.11), channel_id=1, source_target_pairs={{0,2},{1,3},{2,0},{3,1},{4,6},{5,7},{6,4},{7,5},{8,10},{9,11},{10,... | collective-permute-start | bytes 6782984 | tf_op jit(solution)/shard_map/ppermute | solution.py:117
  38.0 295.8 %collective-permute-start.2 = (bf16[23,3,64,256]{3,2,1,0:T(8,128)(2,1)}, bf16[23,3,64,256]{3,2,1,0:T(8,128)(2,1)}, u32[]{:S(2)}, u32[]{:S(2)}) collective-permute-start(bf16[23,3,64,256]{3,2,1,0:T(8,128)(2,1)} %get-tuple-element.12), channel_id=1, source_target_pairs={{0,3},{1,0},{2,1},{3,2},{4,7},{5,4},{6,5},{7,6},{8,11},{9,8},{10,9... | collective-permute-start | bytes 6782984 | tf_op jit(solution)/shard_map/ppermute | solution.py:117

commit v2 on v1

--- a/solution.py
+++ b/solution.py
@@ -34,10 +34,11 @@
     out_ref[:, 0, 0, :, half:] = high_rows.reshape(dests, slots, half).astype(BF16)
 
 
-def synthesise_kernel(order_ref, degree_ref, table_ref, mixed_ref, out_ref, low_pick, high_pick):
+def synthesise_kernel(order_ref, degree_ref, table_ref, *refs):
+    mixed_refs, (out_ref, low_pick, high_pick, held) = refs[:-4], refs[-4:]
     pair = pl.program_id(0)
     rows = table_ref.shape[3]
-    half = mixed_ref.shape[4] // 2
+    half = held.shape[1] // 2
 
     @pl.when(pl.program_id(1) == 0)
     def _():
@@ -48,8 +49,13 @@
         high = jnp.where(degree >= rows - 2 - low, degree + 1, -1)
         high_pick[...] = jnp.where(at == high, 1.0, 0.0).astype(BF16)
 
-    dests, _, _, slots, width = mixed_ref.shape
-    mixed = mixed_ref[:, 0, 0].astype(F32).reshape(dests * slots, width).astype(BF16)
+    for spin, mixed_ref in enumerate(mixed_refs):
+
+        @pl.when(pl.program_id(1) == spin)
+        def _(mixed_ref=mixed_ref):
+            held[...] = mixed_ref[:, :, 0].astype(F32).reshape(held.shape).astype(BF16)
+
+    mixed = held[...]
     low_rows = lax.dot_general(mixed[:, :half], low_pick[...], FIRST, preferred_element_type=F32)
     high_rows = lax.dot_general(mixed[:, half:], high_pick[...], FIRST, preferred_element_type=F32)
     back = jnp.concatenate([low_rows, high_rows], axis=0).astype(BF16)
@@ -61,7 +67,7 @@
 def mix_kernel(slot_count, where_ref, x_ref, *refs):
     weights, out_ref = refs[:-1], refs[-1]
     blocks = len(weights)
-    _, spins, _, items, width = x_ref.shape
+    _, _, items, width = x_ref.shape
     chans = weights[0].shape[2]
     parts = width // chans
     me = where_ref[0]
@@ -69,20 +75,19 @@
 
     @pl.when(live)
     def _():
-        for s in range(spins):
-            held = []
-            for shift in range(blocks):
-                x = x_ref[0, s, lax.rem(me - shift + blocks, blocks)]
-                held.append(
-                    jnp.concatenate([x[:, i * chans:(i + 1) * chans] for i in range(parts)], axis=0)
-                )
-            w = jnp.concatenate([weight[0, s] for weight in weights], axis=0)
-            y = jnp.dot(jnp.concatenate(held, axis=1), w, preferred_element_type=F32).astype(BF16)
-            for g in range(blocks):
-                out_ref[0, s, g] = jnp.concatenate(
-                    [y[i * items:(i + 1) * items, g * chans:(g + 1) * chans] for i in range(parts)],
-                    axis=1,
-                )
+        held = []
+        for shift in range(blocks):
+            x = x_ref[0, lax.rem(me - shift + blocks, blocks)]
+            held.append(
+                jnp.concatenate([x[:, i * chans:(i + 1) * chans] for i in range(parts)], axis=0)
+            )
+        w = jnp.concatenate([weight[0, 0] for weight in weights], axis=0)
+        y = jnp.dot(jnp.concatenate(held, axis=1), w, preferred_element_type=F32).astype(BF16)
+        for g in range(blocks):
+            out_ref[0, lax.rem(g - me + blocks, blocks)] = jnp.concatenate(
+                [y[i * items:(i + 1) * items, g * chans:(g + 1) * chans] for i in range(parts)],
+                axis=1,
+            )
 
     @pl.when(jnp.logical_not(live))
     def _():
@@ -103,18 +108,20 @@
     within = jnp.arange(padded, dtype=jnp.int32)
     slot = jnp.arange(blocks, dtype=jnp.int32)[:, None] * slots + within[None, :]
     real = (within[None, None, :] < slots) & (slot[None] < deg_counts[:, None, None])
-    degree = jnp.where(real, starts[:, None, None] + slot[None], -(1 << 20)).reshape(-1, 1)
+    degree = jnp.where(real, starts[:, None, None] + slot[None], -(1 << 20))
+    sources = lax.rem(me - jnp.arange(blocks, dtype=jnp.int32) + blocks, blocks)
+    degree_back = jnp.take(degree, sources, axis=1).reshape(-1, 1)
+    degree = degree.reshape(-1, 1)
     total = dests * padded
 
+    rings = [[(g, (g + d) % blocks) for g in range(blocks)] for d in range(1, blocks)]
+    rings = [[(g, (g + d) % blocks) for g in range(blocks)] for d in range(1, blocks)]
     sent = []
     for shift in range(1, blocks):
         to = lax.rem(me + shift, blocks)
         sent.append(lax.dynamic_slice_in_dim(mix_weight, to * slots, slots, axis=0))
     degree, *sent = lax.optimization_barrier((degree, *sent))
-    weights = [mix_weight]
-    for shift in range(1, blocks):
-        ring = [(g, (g + shift) % blocks) for g in range(blocks)]
-        weights.append(lax.ppermute(sent[shift - 1], "chan", ring))
+    arrived = [lax.ppermute(sent[d], "chan", rings[d]) for d in range(blocks - 1)]
     table = wigner.transpose(0, 1, 3, 2)
     lines = fields.transpose(0, 1, 3, 4, 5, 2).reshape(pairs, spins, width, cycles)
 
@@ -143,46 +150,66 @@
     received = lax.all_to_all(outgoing, ("order", "chan"), split_axis=0, concat_axis=0, tiled=True)
     received = received.reshape(owners, blocks, pairs, spins, padded, width)
     items = owners * pairs
-    x = received.transpose(4, 3, 1, 0, 2, 5).reshape(padded, spins, blocks, items, width)
+    x_shape = (padded, blocks, items, width)
 
     def block_at(k):
         return jnp.minimum(k, slots - 1)
 
-    weight_block = (1, spins, chans, mix_weight.shape[3])
-    weight_specs = [pl.BlockSpec(weight_block, lambda k, w: (w[0] * slots + block_at(k), 0, 0, 0))]
-    weight_specs += [pl.BlockSpec(weight_block, lambda k, w: (block_at(k), 0, 0, 0))] * (blocks - 1)
-    x_spec = pl.BlockSpec((1, spins, blocks, items, width), lambda k, w: (k, 0, 0, 0, 0))
-    mixed = pl.pallas_call(
-        functools.partial(mix_kernel, slots),
-        out_shape=jax.ShapeDtypeStruct(x.shape, BF16),
-        grid_spec=pltpu.PrefetchScalarGridSpec(
-            num_scalar_prefetch=1,
-            grid=(padded,),
-            in_specs=[x_spec] + weight_specs,
-            out_specs=x_spec,
-        ),
-        compiler_params=PARAMS,
-        name="mix",
-    )(me.reshape(1).astype(jnp.int32), x, *weights)
-
-    mixed = mixed.reshape(padded, spins, blocks, owners, pairs, width).transpose(3, 2, 4, 1, 0, 5)
-    mixed = mixed.reshape(dests, pairs, spins, padded, width)
-    returned = lax.all_to_all(mixed, ("order", "chan"), split_axis=0, concat_axis=0, tiled=True)
-
+    crossings, returned = [], []
+    for spin in range(spins):
+        x = received[:, :, :, spin].transpose(3, 1, 0, 2, 4).reshape(x_shape)
+        block = (1, 1, chans, mix_weight.shape[3])
+        specs = [
+            pl.BlockSpec(block, lambda k, w, spin=spin: (w[0] * slots + block_at(k), spin, 0, 0))
+        ]
+        specs += [
+            pl.BlockSpec(block, lambda k, w, spin=spin: (block_at(k), spin, 0, 0))
+        ] * (blocks - 1)
+        x_spec = pl.BlockSpec((1,) + x_shape[1:], lambda k, w: (k, 0, 0, 0))
+        mixed = pl.pallas_call(
+            functools.partial(mix_kernel, slots),
+            out_shape=jax.ShapeDtypeStruct(x_shape, BF16),
+            grid_spec=pltpu.PrefetchScalarGridSpec(
+                num_scalar_prefetch=1, grid=(padded,), in_specs=[x_spec] + specs, out_specs=x_spec
+            ),
+            compiler_params=PARAMS,
+            cost_estimate=pl.CostEstimate(
+                flops=2 * padded * 4 * items * (blocks * chans) ** 2,
+                bytes_accessed=4 * padded * blocks * items * width,
+                transcendentals=0,
+            ),
+            name="mix",
+        )(me.reshape(1).astype(jnp.int32), x, mix_weight, *arrived)
+        mixed = mixed.reshape(padded, blocks, owners, pairs, width).transpose(1, 2, 3, 0, 4)
+        crossed = [mixed[0]]
+        for shift in range(1, blocks):
+            crossed.append(lax.ppermute(mixed[shift], "chan", rings[shift - 1]))
+        crossings.append(crossed)
+    for spin in range(spins):
+        crossed = crossings[spin]
+        if spin + 1 < spins:
+            later = crossings[spin + 1]
+            *crossed, later[0] = lax.optimization_barrier((*crossed, later[0]))
+        crossed = jnp.stack(crossed, axis=1)
+        returned.append(lax.all_to_all(crossed, "order", split_axis=0, concat_axis=0, tiled=True))
+
+    back_spec = pl.BlockSpec((owners, blocks, 1, padded, width), lambda p, s, o: (0, 0, p, 0, 0))
     out = pl.pallas_call(
         synthesise_kernel,
         out_shape=jax.ShapeDtypeStruct((pairs, spins, width, cycles), BF16),
         grid_spec=pltpu.PrefetchScalarGridSpec(
             num_scalar_prefetch=1,
             grid=(pairs, spins),
-            in_specs=[pl.BlockSpec((total, 1), lambda p, s, o: (0, 0)), table_spec, moved_spec],
+            in_specs=[pl.BlockSpec((total, 1), lambda p, s, o: (0, 0)), table_spec]
+            + [back_spec] * spins,
             out_specs=field_spec,
-            scratch_shapes=[pltpu.VMEM((total, rows), BF16)] * 2,
+            scratch_shapes=[pltpu.VMEM((total, rows), BF16)] * 2
+            + [pltpu.VMEM((total, width), BF16)],
         ),
         compiler_params=PARAMS,
         cost_estimate=cost,
         name="synthesise",
-    )(pair_orders, degree, table, returned)
+    )(pair_orders, degree_back, table, *returned)
     return out.reshape(pairs, spins, 2, 2, chans, cycles).transpose(0, 1, 5, 2, 3, 4)
 
 

time: 498 us -> 572 us (1.15)
  blocking collectives: 108 us -> 0 us
  waiting for transfers between devices: 280 us -> 382 us
  starting transfers between devices: 9.28 us -> 53.7 us
  Pallas kernels: 55.9 us -> 78.7 us
  other arithmetic: 2.3 us -> 8.68 us
    all_to_all x1 -> x0, blocking collectives: 108 us -> none  [per_device(): lax.all_to_all(mixed, ('order', 'chan'), split_axis=0, concat_axis=0, til...]
    all_to_all x0 -> x3, waiting for transfers between devices: none -> 55.8 us  [per_device(): lax.all_to_all(crossed, 'order', split_axis=0, concat_axis=0, tiled=True)]
    ppermute x3 -> x12, waiting for transfers between devices: 81.5 us -> 128 us  [the longest x3 85.4 us: per_device(): lax.ppermute(sent[d], 'chan', rings[d])]
    ppermute x3 -> x12, starting transfers between devices: 3.29 us -> 36.1 us  [the longest x9 32.8 us: per_device(): crossed.append(lax.ppermute(mixed[shift], 'chan', rings[shift - 1]))]
    pallas_call x1 -> x3, Pallas kernels: 19.5 us -> 41.7 us  [per_device(): pl.pallas_call(functools.partial(mix_kernel, slots), out_shape=jax.ShapeD...]
    reshape x4 -> x3, local copies, waits for them, and re-layouts: 28.9 us -> 10.5 us  [per_device(): x = received[:, :, :, spin].transpose(3, 1, 0, 2, 4).reshape(x_shape)]
    all_to_all x0 -> x3, starting transfers between devices: none -> 11.6 us  [per_device(): lax.all_to_all(crossed, 'order', split_axis=0, concat_axis=0, tiled=True)]
    unnamed x4 -> x23, local copies, waits for them, and re-layouts: 2.19 us -> 10.7 us
  transfers between devices with their start and end apart: 4 -> 16, of which waited for: 3 -> 11; matrix products, arithmetic and copies ran while one was open for 3% -> 5% of each run, Pallas kernels for 0% -> 5%
where the time goes in v2:
time: 572 us; the launch traced here: 565 us
  waiting for transfers between devices  382 us (67%)
  Pallas kernels  78.7 us (14%)
  starting transfers between devices  53.7 us (9%)
  local copies, waits for them, and re-layouts  41.9 us (7%)
  other arithmetic  8.68 us (2%)
    all_to_all x1, waiting for transfers between devices, per_device(): lax.all_to_all(outgoing, ('order', 'chan'), split_axis=0, concat_axis=0,...  198 us
    ppermute x3, waiting for transfers between devices, per_device(): lax.ppermute(sent[d], 'chan', rings[d])  85.4 us
    all_to_all x3, waiting for transfers between devices, per_device(): lax.all_to_all(crossed, 'order', split_axis=0, concat_axis=0, tiled=True)  55.8 us
    ppermute x9, waiting for transfers between devices, per_device(): crossed.append(lax.ppermute(mixed[shift], 'chan', rings[shift - 1]))  43 us
    pallas_call x3, Pallas kernels, per_device(): pl.pallas_call(functools.partial(mix_kernel, slots), out_shape=jax.ShapeD...  41.7 us
    ppermute x9, starting transfers between devices, per_device(): crossed.append(lax.ppermute(mixed[shift], 'chan', rings[shift - 1]))  32.8 us
    pallas_call x1, Pallas kernels, per_device(): pl.pallas_call(analyse_kernel, out_shape=moved, grid_spec=pltpu.PrefetchS...  18.9 us
    pallas_call x1, Pallas kernels, per_device(): pl.pallas_call(synthesise_kernel, out_shape=jax.ShapeDtypeStruct((pairs,...  18 us
  transfers between devices with their start and end apart: 16, of which 11 were waited for; matrix products, arithmetic and copies ran while one was open for 5% of the time, Pallas kernels for 5%

profile of v2, /device:TPU:16, one launch (start us, length us, event | category | flops | bytes accessed | tf_op | source)
XLA Modules:
  0.0 565.4 jit_solution(3184588815470327413)
XLA Ops:
  0.1 0.8 reduce-window.9
  3.0 6.0 %constant_dynamic-slice_fusion = (bf16[23,3,64,256]{3,2,1,0:T(8,128)(2,1)}, bf16[23,3,64,256]{3,2,1,0:T(8,128)(2,1)}, bf16[23,3,64,256]{3,2,1,0:T(8,128)(2,1)}) fusion(bf16[92,3,64,256]{3,2,1,0:T(8,128)(2,1)} %refs_0_.5, s32[]{:T(128)S(6)} %select_n.61, s32[]{:T(128)S(6)} %select_n.60, s32[]{:T(128)S(6)} %select_n.59), kind=kLoop, calls=%fused_computation.30 | loop fusion | bytes 13565964 | tf_op jit(solution)/shard_map/dynamic_slice | solution.py:122
  9.2 18.9 %analyse.1 = bf16[32,4,3,24,256]{4,3,2,1,0:T(8,128)(2,1)S(1)} custom-call(s32[4]{0:T(128)S(1)} %copy-done.4, s32[768,1]{1,0:T(8,128)S(1)} %copy.23.degree_ref, bf16[4,3,720,721]{3,2,1,0:T(8,128)(2,1)} %bitcast.105, bf16[4,3,256,720]{3,2,1,0:T(8,128)(2,1)} %bitcast.107), custom_call_target="tpu_custom_call" | custom-call | flops 6378946560 | bytes 24917760 | tf_op jit(solution)/shard_map/analyse/pallas_call | solution.py:135
  28.1 2.2 copy-done.3
  30.3 6.0 %all-to-all-start = ((bf16[32,4,3,24,256]{4,3,2,1,0:T(8,128)(2,1)}), bf16[32,4,3,24,256]{4,3,2,1,0:T(8,128)(2,1)}, u32[]{:S(2)}, u32[]{:S(2)}) async-start(bf16[32,4,3,24,256]{4,3,2,1,0:T(8,128)(2,1)} %copy-done.3), calls=%async_computation | async-start | bytes 9437184 | tf_op jit(solution)/shard_map/all_to_all | solution.py:150
  36.3 1.6 collective-permute-start
  38.4 1.2 collective-permute-start.2
  39.6 198.1 %all-to-all-done = bf16[32,4,3,24,256]{4,3,2,1,0:T(8,128)(2,1)} async-done(((bf16[32,4,3,24,256]{4,3,2,1,0:T(8,128)(2,1)}), bf16[32,4,3,24,256]{4,3,2,1,0:T(8,128)(2,1)}, u32[]{:S(2)}, u32[]{:S(2)}) %all-to-all-start) | async-done | bytes 4718624 | tf_op jit(solution)/shard_map/all_to_all | solution.py:150
  237.7 4.1 fusion.3
  241.8 3.5 copy_bitcast_fusion
  245.3 3.5 reshape.223.x_ref
  248.8 37.7 %collective-permute-done.refs_1_ = bf16[23,3,64,256]{3,2,1,0:T(8,128)(2,1)S(1)} collective-permute-done((bf16[23,3,64,256]{3,2,1,0:T(8,128)(2,1)}, bf16[23,3,64,256]{3,2,1,0:T(8,128)(2,1)S(1)}, u32[]{:S(2)}, u32[]{:S(2)}) %collective-permute-start) | collective-permute-done | bytes 2261024 | tf_op jit(solution)/shard_map/ppermute | solution.py:124
  286.5 47.7 %collective-permute-done.2.refs_3_ = bf16[23,3,64,256]{3,2,1,0:T(8,128)(2,1)} collective-permute-done((bf16[23,3,64,256]{3,2,1,0:T(8,128)(2,1)}, bf16[23,3,64,256]{3,2,1,0:T(8,128)(2,1)}, u32[]{:S(2)}, u32[]{:S(2)}) %collective-permute-start.2) | collective-permute-done | bytes 2261024 | tf_op jit(solution)/shard_map/ppermute | solution.py:124
  334.2 1.4 copy-done
  335.6 13.9 %mix.4 = bf16[24,4,32,256]{3,2,1,0:T(8,128)(2,1)S(1)} custom-call(s32[1]{0:T(128)} %bitcast.5.where_ref, bf16[24,4,32,256]{3,2,1,0:T(8,128)(2,1)S(1)} %copy-done, bf16[92,3,64,256]{3,2,1,0:T(8,128)(2,1)} %refs_0_.5, bf16[23,3,64,256]{3,2,1,0:T(8,128)(2,1)S(1)} %collective-permute-done.refs_1_, bf16[23,3,64,256]{3,2,1,0:T(8,128)(2,1)} %collective-permute-done.1.refs_2_, ...), custom_call_target="tpu_custom_call" | custom-call | flops 402653184 | bytes 3145728 | tf_op jit(solution)/shard_map/mix/pallas_call | solution.py:169
  349.5 0.9 copy.27
  350.4 1.0 slice_bitcast_fusion.4
  351.4 1.9 collective-permute-start.6
  353.3 2.0 copy.46
  355.4 3.5 reshape.221.x_ref
  358.9 1.4 copy-done.2
  360.3 13.9 %mix.3 = bf16[24,4,32,256]{3,2,1,0:T(8,128)(2,1)S(1)} custom-call(s32[1]{0:T(128)} %bitcast.5.where_ref, bf16[24,4,32,256]{3,2,1,0:T(8,128)(2,1)S(1)} %copy-done.2, bf16[92,3,64,256]{3,2,1,0:T(8,128)(2,1)} %refs_0_.5, bf16[23,3,64,256]{3,2,1,0:T(8,128)(2,1)S(1)} %collective-permute-done.refs_1_, bf16[23,3,64,256]{3,2,1,0:T(8,128)(2,1)} %collective-permute-done.1.refs_2_, ...), custom_call_target="tpu_custom_call" | custom-call | flops 402653184 | bytes 3145728 | tf_op jit(solution)/shard_map/mix/pallas_call | solution.py:169
  374.2 0.9 copy.25
  375.1 1.0 slice_bitcast_fusion.8
  376.9 2.1 collective-permute-start.4
  379.0 2.1 collective-permute-start.5
  381.1 3.5 reshape.225.x_ref
  384.6 1.4 copy-done.1
  386.0 13.9 %mix.5 = bf16[24,4,32,256]{3,2,1,0:T(8,128)(2,1)S(1)} custom-call(s32[1]{0:T(128)} %bitcast.5.where_ref, bf16[24,4,32,256]{3,2,1,0:T(8,128)(2,1)S(1)} %copy-done.1, bf16[92,3,64,256]{3,2,1,0:T(8,128)(2,1)} %refs_0_.5, bf16[23,3,64,256]{3,2,1,0:T(8,128)(2,1)S(1)} %collective-permute-done.refs_1_, bf16[23,3,64,256]{3,2,1,0:T(8,128)(2,1)} %collective-permute-done.1.refs_2_, ...), custom_call_target="tpu_custom_call" | custom-call | flops 402653184 | bytes 3145728 | tf_op jit(solution)/shard_map/mix/pallas_call | solution.py:169
  399.9 0.9 copy.32
  400.8 1.0 collective-permute-start.7
  401.9 0.9 copy-done.6
  403.3 18.0 %collective-permute-done.3 = bf16[8,4,24,256]{3,2,1,0:T(8,128)(2,1)} collective-permute-done((bf16[8,4,24,256]{3,2,1,0:T(8,128)(2,1)}, bf16[8,4,24,256]{3,2,1,0:T(8,128)(2,1)}, u32[]{:S(2)}, u32[]{:S(2)}) %collective-permute-start.3) | collective-permute-done | bytes 393248 | tf_op jit(solution)/shard_map/ppermute | solution.py:186
  422.3 23.9 %collective-permute-start.11 = (bf16[8,4,24,256]{3,2,1,0:T(8,128)(2,1)S(1)}, bf16[8,4,24,256]{3,2,1,0:T(8,128)(2,1)S(1)}, u32[]{:S(2)}, u32[]{:S(2)}) collective-permute-start(bf16[8,4,24,256]{3,2,1,0:T(8,128)(2,1)S(1)} %get-tuple-element.40), channel_id=1, source_target_pairs={{0,3},{1,0},{2,1},{3,2},{4,7},{5,4},{6,5},{7,6},{8,11},{9,8},{10,9... | collective-permute-start | bytes 1179656 | tf_op jit(solution)/shard_map/ppermute | solution.py:186
  446.2 8.5 %collective-permute-done.8 = bf16[8,4,24,256]{3,2,1,0:T(8,128)(2,1)S(1)} collective-permute-done((bf16[8,4,24,256]{3,2,1,0:T(8,128)(2,1)S(1)}, bf16[8,4,24,256]{3,2,1,0:T(8,128)(2,1)S(1)}, u32[]{:S(2)}, u32[]{:S(2)}) %collective-permute-start.8) | collective-permute-done | bytes 393248 | tf_op jit(solution)/shard_map/ppermute | solution.py:186
  455.5 8.8 %collective-permute-done.9 = bf16[8,4,24,256]{3,2,1,0:T(8,128)(2,1)S(1)} collective-permute-done((bf16[8,4,24,256]{3,2,1,0:T(8,128)(2,1)S(1)}, bf16[8,4,24,256]{3,2,1,0:T(8,128)(2,1)S(1)}, u32[]{:S(2)}, u32[]{:S(2)}) %collective-permute-start.9) | collective-permute-done | bytes 393248 | tf_op jit(solution)/shard_map/ppermute | solution.py:186
  464.3 7.2 %collective-permute-done.11 = bf16[8,4,24,256]{3,2,1,0:T(8,128)(2,1)S(1)} collective-permute-done((bf16[8,4,24,256]{3,2,1,0:T(8,128)(2,1)S(1)}, bf16[8,4,24,256]{3,2,1,0:T(8,128)(2,1)S(1)}, u32[]{:S(2)}, u32[]{:S(2)}) %collective-permute-start.11) | collective-permute-done | bytes 393248 | tf_op jit(solution)/shard_map/ppermute | solution.py:186
  471.4 1.3 pad_maximum_fusion.2
  472.8 3.7 all-to-all-start.3
  476.5 2.4 pad_maximum_fusion.1
  478.9 18.6 %all-to-all-done.3.refs_2_ = bf16[8,4,4,24,256]{4,3,2,1,0:T(8,128)(2,1)S(1)} async-done(((bf16[8,4,4,24,256]{4,3,2,1,0:T(8,128)(2,1)}), bf16[8,4,4,24,256]{4,3,2,1,0:T(8,128)(2,1)S(1)}, u32[]{:S(2)}, u32[]{:S(2)}) %all-to-all-start.3) | async-done | bytes 1572896 | tf_op jit(solution)/shard_map/all_to_all | solution.py:194
  497.5 3.6 all-to-all-start.2
  501.0 2.6 pad_maximum_fusion
  503.6 18.4 %all-to-all-done.2.refs_1_ = bf16[8,4,4,24,256]{4,3,2,1,0:T(8,128)(2,1)S(1)} async-done(((bf16[8,4,4,24,256]{4,3,2,1,0:T(8,128)(2,1)}), bf16[8,4,4,24,256]{4,3,2,1,0:T(8,128)(2,1)S(1)}, u32[]{:S(2)}, u32[]{:S(2)}) %all-to-all-start.2) | async-done | bytes 1572896 | tf_op jit(solution)/shard_map/all_to_all | solution.py:194
  522.0 4.3 all-to-all-start.1
  527.6 0.9 select_n.63.degree_ref
  528.5 18.8 %all-to-all-done.1.refs_0_ = bf16[8,4,4,24,256]{4,3,2,1,0:T(8,128)(2,1)} async-done(((bf16[8,4,4,24,256]{4,3,2,1,0:T(8,128)(2,1)}), bf16[8,4,4,24,256]{4,3,2,1,0:T(8,128)(2,1)}, u32[]{:S(2)}, u32[]{:S(2)}) %all-to-all-start.1) | async-done | bytes 1572896 | tf_op jit(solution)/shard_map/all_to_all | solution.py:194
  547.3 18.0 %synthesise.1 = bf16[4,3,256,720]{3,2,1,0:T(8,128)(2,1)} custom-call(s32[4]{0:T(128)S(1)} %copy-done.4, s32[768,1]{1,0:T(8,128)S(1)} %select_n.63.degree_ref, bf16[4,3,720,721]{3,2,1,0:T(8,128)(2,1)} %bitcast.106, bf16[8,4,4,24,256]{4,3,2,1,0:T(8,128)(2,1)} %all-to-all-done.1.refs_0_, bf16[8,4,4,24,256]{4,3,2,1,0:T(8,128)(2,1)S(1)} %all-to-all-done.2.refs_1_, ...), custom_call_target="tpu_custom_call" | custom-call | flops 6378946560 | bytes 24917760 | tf_op jit(solution)/shard_map/synthesise/pallas_call | solution.py:197
  (43 shorter events, 7.3 us)
Async XLA Ops:
  2.3 0.6 copy-start.9
  3.0 6.2 %copy-start.4 = (s32[4]{0:T(128)S(1)}, s32[4]{0:T(128)}, u32[]{:S(2)}) copy-start(s32[4]{0:T(128)} %order_ref.3) | copy-start | bytes 52
  28.1 2.2 copy-start.3
  30.3 207.4 %all-to-all-start = ((bf16[32,4,3,24,256]{4,3,2,1,0:T(8,128)(2,1)}), bf16[32,4,3,24,256]{4,3,2,1,0:T(8,128)(2,1)}, u32[]{:S(2)}, u32[]{:S(2)}) async-start(bf16[32,4,3,24,256]{4,3,2,1,0:T(8,128)(2,1)} %copy-done.3), calls=%async_computation | async-start | bytes 9437184 | tf_op jit(solution)/shard_map/all_to_all | solution.py:150
  36.3 250.2 %collective-permute-start = (bf16[23,3,64,256]{3,2,1,0:T(8,128)(2,1)}, bf16[23,3,64,256]{3,2,1,0:T(8,128)(2,1)S(1)}, u32[]{:S(2)}, u32[]{:S(2)}) collective-permute-start(bf16[23,3,64,256]{3,2,1,0:T(8,128)(2,1)} %get-tuple-element.20), channel_id=1, source_target_pairs={{0,1},{1,2},{2,3},{3,0},{4,5},{5,6},{6,7},{7,4},{8,9},{9,10},{10,1... | collective-permute-start | bytes 6782984 | tf_op jit(solution)/shard_map/ppermute | solution.py:124
  37.9 248.6 %collective-permute-start.1 = (bf16[23,3,64,256]{3,2,1,0:T(8,128)(2,1)}, bf16[23,3,64,256]{3,2,1,0:T(8,128)(2,1)}, u32[]{:S(2)}, u32[]{:S(2)}) collective-permute-start(bf16[23,3,64,256]{3,2,1,0:T(8,128)(2,1)} %get-tuple-element.21), channel_id=1, source_target_pairs={{0,2},{1,3},{2,0},{3,1},{4,6},{5,7},{6,4},{7,5},{8,10},{9,11},{10,... | collective-permute-start | bytes 6782984 | tf_op jit(solution)/shard_map/ppermute | solution.py:124
  38.4 295.8 %collective-permute-start.2 = (bf16[23,3,64,256]{3,2,1,0:T(8,128)(2,1)}, bf16[23,3,64,256]{3,2,1,0:T(8,128)(2,1)}, u32[]{:S(2)}, u32[]{:S(2)}) collective-permute-start(bf16[23,3,64,256]{3,2,1,0:T(8,128)(2,1)} %get-tuple-element.22), channel_id=1, source_target_pairs={{0,3},{1,0},{2,1},{3,2},{4,7},{5,4},{6,5},{7,6},{8,11},{9,8},{10,9... | collective-permute-start | bytes 6782984 | tf_op jit(solution)/shard_map/ppermute | solution.py:124
  334.2 1.4 copy-start
  350.4 2.9 copy-start.5
  351.4 50.5 %collective-permute-start.6 = (bf16[8,4,24,256]{3,2,1,0:T(8,128)(2,1)}, bf16[8,4,24,256]{3,2,1,0:T(8,128)(2,1)}, u32[]{:S(2)}, u32[]{:S(2)}) collective-permute-start(bf16[8,4,24,256]{3,2,1,0:T(8,128)(2,1)} %get-tuple-element.45), channel_id=1, source_target_pairs={{0,1},{1,2},{2,3},{3,0},{4,5},{5,6},{6,7},{7,4},{8,9},{9,10},{10,1... | collective-permute-start | bytes 1179656 | tf_op jit(solution)/shard_map/ppermute | solution.py:186
  358.9 1.4 copy-start.2
  376.1 45.2 %collective-permute-start.3 = (bf16[8,4,24,256]{3,2,1,0:T(8,128)(2,1)}, bf16[8,4,24,256]{3,2,1,0:T(8,128)(2,1)}, u32[]{:S(2)}, u32[]{:S(2)}) collective-permute-start(bf16[8,4,24,256]{3,2,1,0:T(8,128)(2,1)} %get-tuple-element.49), channel_id=1, source_target_pairs={{0,1},{1,2},{2,3},{3,0},{4,5},{5,6},{6,7},{7,4},{8,9},{9,10},{10,1... | collective-permute-start | bytes 1179656 | tf_op jit(solution)/shard_map/ppermute | solution.py:186
  376.9 44.4 %collective-permute-start.4 = (bf16[8,4,24,256]{3,2,1,0:T(8,128)(2,1)}, bf16[8,4,24,256]{3,2,1,0:T(8,128)(2,1)}, u32[]{:S(2)}, u32[]{:S(2)}) collective-permute-start(bf16[8,4,24,256]{3,2,1,0:T(8,128)(2,1)} %get-tuple-element.48), channel_id=1, source_target_pairs={{0,2},{1,3},{2,0},{3,1},{4,6},{5,7},{6,4},{7,5},{8,10},{9,11},{10,... | collective-permute-start | bytes 1179656 | tf_op jit(solution)/shard_map/ppermute | solution.py:186
  379.0 43.3 %collective-permute-start.5 = (bf16[8,4,24,256]{3,2,1,0:T(8,128)(2,1)}, bf16[8,4,24,256]{3,2,1,0:T(8,128)(2,1)}, u32[]{:S(2)}, u32[]{:S(2)}) collective-permute-start(bf16[8,4,24,256]{3,2,1,0:T(8,128)(2,1)} %get-tuple-element.47), channel_id=1, source_target_pairs={{0,3},{1,0},{2,1},{3,2},{4,7},{5,4},{6,5},{7,6},{8,11},{9,8},{10,9... | collective-permute-start | bytes 1179656 | tf_op jit(solution)/shard_map/ppermute | solution.py:186
  384.6 1.4 copy-start.1
  400.8 45.4 %collective-permute-start.7 = (bf16[8,4,24,256]{3,2,1,0:T(8,128)(2,1)}, bf16[8,4,24,256]{3,2,1,0:T(8,128)(2,1)S(1)}, u32[]{:S(2)}, u32[]{:S(2)}) collective-permute-start(bf16[8,4,24,256]{3,2,1,0:T(8,128)(2,1)} %get-tuple-element.44), channel_id=1, source_target_pairs={{0,2},{1,3},{2,0},{3,1},{4,6},{5,7},{6,4},{7,5},{8,10},{9,11},{10,... | collective-permute-start | bytes 1179656 | tf_op jit(solution)/shard_map/ppermute | solution.py:186
  401.8 1.0 copy-start.6
  402.8 52.0 %collective-permute-start.8 = (bf16[8,4,24,256]{3,2,1,0:T(8,128)(2,1)S(1)}, bf16[8,4,24,256]{3,2,1,0:T(8,128)(2,1)S(1)}, u32[]{:S(2)}, u32[]{:S(2)}) collective-permute-start(bf16[8,4,24,256]{3,2,1,0:T(8,128)(2,1)S(1)} %copy-done.6), channel_id=1, source_target_pairs={{0,3},{1,0},{2,1},{3,2},{4,7},{5,4},{6,5},{7,6},{8,11},{9,8},{10,9... | collective-permute-start | bytes 1179656 | tf_op jit(solution)/shard_map/ppermute | solution.py:186
  421.3 43.0 %collective-permute-start.9 = (bf16[8,4,24,256]{3,2,1,0:T(8,128)(2,1)S(1)}, bf16[8,4,24,256]{3,2,1,0:T(8,128)(2,1)S(1)}, u32[]{:S(2)}, u32[]{:S(2)}) collective-permute-start(bf16[8,4,24,256]{3,2,1,0:T(8,128)(2,1)S(1)} %get-tuple-element.39), channel_id=1, source_target_pairs={{0,1},{1,2},{2,3},{3,0},{4,5},{5,6},{6,7},{7,4},{8,9},{9,10},{10,1... | collective-permute-start | bytes 1179656 | tf_op jit(solution)/shard_map/ppermute | solution.py:186
  421.3 43.0 %collective-permute-start.10 = (bf16[8,4,24,256]{3,2,1,0:T(8,128)(2,1)S(1)}, bf16[8,4,24,256]{3,2,1,0:T(8,128)(2,1)S(1)}, u32[]{:S(2)}, u32[]{:S(2)}) collective-permute-start(bf16[8,4,24,256]{3,2,1,0:T(8,128)(2,1)S(1)} %get-tuple-element.41), channel_id=1, source_target_pairs={{0,2},{1,3},{2,0},{3,1},{4,6},{5,7},{6,4},{7,5},{8,10},{9,11},{10,... | collective-permute-start | bytes 1179656 | tf_op jit(solution)/shard_map/ppermute | solution.py:186
  422.3 49.2 %collective-permute-start.11 = (bf16[8,4,24,256]{3,2,1,0:T(8,128)(2,1)S(1)}, bf16[8,4,24,256]{3,2,1,0:T(8,128)(2,1)S(1)}, u32[]{:S(2)}, u32[]{:S(2)}) collective-permute-start(bf16[8,4,24,256]{3,2,1,0:T(8,128)(2,1)S(1)} %get-tuple-element.40), channel_id=1, source_target_pairs={{0,3},{1,0},{2,1},{3,2},{4,7},{5,4},{6,5},{7,6},{8,11},{9,8},{10,9... | collective-permute-start | bytes 1179656 | tf_op jit(solution)/shard_map/ppermute | solution.py:186
  454.8 0.7 copy-start.7
  472.8 3.7 copy-start.8
  472.8 24.7 %all-to-all-start.3 = ((bf16[8,4,4,24,256]{4,3,2,1,0:T(8,128)(2,1)}), bf16[8,4,4,24,256]{4,3,2,1,0:T(8,128)(2,1)S(1)}, u32[]{:S(2)}, u32[]{:S(2)}) async-start(bf16[8,4,4,24,256]{4,3,2,1,0:T(8,128)(2,1)} %pad_maximum_fusion.2), calls=%async_computation.3 | async-start | bytes 3145728 | tf_op jit(solution)/shard_map/all_to_all | solution.py:194
  497.5 24.5 %all-to-all-start.2 = ((bf16[8,4,4,24,256]{4,3,2,1,0:T(8,128)(2,1)}), bf16[8,4,4,24,256]{4,3,2,1,0:T(8,128)(2,1)S(1)}, u32[]{:S(2)}, u32[]{:S(2)}) async-start(bf16[8,4,4,24,256]{4,3,2,1,0:T(8,128)(2,1)} %pad_maximum_fusion.1), calls=%async_computation.2 | async-start | bytes 3145728 | tf_op jit(solution)/shard_map/all_to_all | solution.py:194
  503.6 22.7 %copy-start.10 = (s32[8,4,24]{2,0,1:T(8,128)S(1)}, s32[8,4,24]{2,0,1:T(8,128)}, u32[]{:S(2)}) copy-start(s32[8,4,24]{2,0,1:T(8,128)} %copy-done.9) | copy-start | bytes 9220
  522.0 25.3 %all-to-all-start.1 = ((bf16[8,4,4,24,256]{4,3,2,1,0:T(8,128)(2,1)}), bf16[8,4,4,24,256]{4,3,2,1,0:T(8,128)(2,1)}, u32[]{:S(2)}, u32[]{:S(2)}) async-start(bf16[8,4,4,24,256]{4,3,2,1,0:T(8,128)(2,1)} %pad_maximum_fusion), calls=%async_computation.1 | async-start | bytes 3145728 | tf_op jit(solution)/shard_map/all_to_all | solution.py:194

commit v3 on v1

--- a/solution.py
+++ b/solution.py
@@ -143,7 +143,7 @@
     received = lax.all_to_all(outgoing, ("order", "chan"), split_axis=0, concat_axis=0, tiled=True)
     received = received.reshape(owners, blocks, pairs, spins, padded, width)
     items = owners * pairs
-    x = received.transpose(4, 3, 1, 0, 2, 5).reshape(padded, spins, blocks, items, width)
+    x = received.transpose(4, 3, 1, 2, 0, 5).reshape(padded, spins, blocks, items, width)
 
     def block_at(k):
         return jnp.minimum(k, slots - 1)
@@ -165,7 +165,7 @@
         name="mix",
     )(me.reshape(1).astype(jnp.int32), x, *weights)
 
-    mixed = mixed.reshape(padded, spins, blocks, owners, pairs, width).transpose(3, 2, 4, 1, 0, 5)
+    mixed = mixed.reshape(padded, spins, blocks, pairs, owners, width).transpose(4, 2, 3, 1, 0, 5)
     mixed = mixed.reshape(dests, pairs, spins, padded, width)
     returned = lax.all_to_all(mixed, ("order", "chan"), split_axis=0, concat_axis=0, tiled=True)
 

time: 498 us -> 488 us (0.980)
  local copies, waits for them, and re-layouts: 37.5 us -> 20.7 us
  waiting for transfers between devices: 280 us -> 287 us
    reshape x3 -> x1, local copies, waits for them, and re-layouts: 21.6 us -> 5.01 us  [per_device(): mixed.reshape(padded, spins, blocks, pairs, owners, width)]
    ppermute x3, waiting for transfers between devices: 81.5 us -> 89.2 us  [per_device(): weights.append(lax.ppermute(sent[shift - 1], 'chan', ring))]
  transfers between devices with their start and end apart: 4 -> 4, of which waited for: 3 -> 3; matrix products, arithmetic and copies ran while one was open for 3% -> 1% of each run, Pallas kernels for 0% -> 0%
where the time goes in v3:
time: 488 us; the launch traced here: 484 us
  waiting for transfers between devices  287 us (59%)
  blocking collectives  108 us (22%)
  Pallas kernels  55.9 us (11%)
  local copies, waits for them, and re-layouts  20.7 us (4%)
  starting transfers between devices  9.28 us (2%)
    all_to_all x1, waiting for transfers between devices, per_device(): lax.all_to_all(outgoing, ('order', 'chan'), split_axis=0, concat_axis=0,...  198 us
    all_to_all x1, blocking collectives, per_device(): lax.all_to_all(mixed, ('order', 'chan'), split_axis=0, concat_axis=0, til...  108 us
    ppermute x3, waiting for transfers between devices, per_device(): weights.append(lax.ppermute(sent[shift - 1], 'chan', ring))  89.2 us
    pallas_call x1, Pallas kernels, per_device(): pl.pallas_call(functools.partial(mix_kernel, slots), out_shape=jax.ShapeD...  19.5 us
    pallas_call x1, Pallas kernels, per_device(): pl.pallas_call(analyse_kernel, out_shape=moved, grid_spec=pltpu.PrefetchS...  18.9 us
    pallas_call x1, Pallas kernels, per_device(): pl.pallas_call(synthesise_kernel, out_shape=jax.ShapeDtypeStruct((pairs,...  17.5 us
  transfers between devices with their start and end apart: 4, of which 3 were waited for; matrix products, arithmetic and copies ran while one was open for 1% of the time, Pallas kernels for 0%

profile of v3, /device:TPU:16, one launch (start us, length us, event | category | flops | bytes accessed | tf_op | source)
XLA Modules:
  0.0 484.1 jit_solution(6073403958740670139)
XLA Ops:
  0.0 0.8 reduce-window.9
  0.8 0.7 bitcast_subtract_fusion
  1.5 0.1 iota_add_fusion
  1.6 0.7 add_select_fusion
  2.3 0.1 select_n.24
  2.4 0.0 copy-start.1
  2.4 6.0 %constant_dynamic-slice_fusion = (bf16[23,3,64,256]{3,2,1,0:T(8,128)(2,1)}, bf16[23,3,64,256]{3,2,1,0:T(8,128)(2,1)}, bf16[23,3,64,256]{3,2,1,0:T(8,128)(2,1)}) fusion(bf16[92,3,64,256]{3,2,1,0:T(8,128)(2,1)} %refs_0_.1, s32[]{:T(128)S(6)} %select_n.27, s32[]{:T(128)S(6)} %select_n.26, s32[]{:T(128)S(6)} %select_n.25), kind=kLoop, calls=%fused_computation.3 | loop fusion | bytes 13565964 | tf_op jit(solution)/shard_map/dynamic_slice | solution.py:112
  8.5 0.2 copy.11.degree_ref
  8.6 0.0 copy-done.1
  8.7 18.9 %analyse.1 = bf16[32,4,3,24,256]{4,3,2,1,0:T(8,128)(2,1)S(1)} custom-call(s32[4]{0:T(128)S(1)} %copy-done.1, s32[768,1]{1,0:T(8,128)S(1)} %copy.11.degree_ref, bf16[4,3,720,721]{3,2,1,0:T(8,128)(2,1)} %bitcast.25, bf16[4,3,256,720]{3,2,1,0:T(8,128)(2,1)} %bitcast.27), custom_call_target="tpu_custom_call" | custom-call | flops 6378946560 | bytes 24917760 | tf_op jit(solution)/shard_map/analyse/pallas_call | solution.py:128
  27.5 0.0 copy-start
  27.6 2.2 copy-done
  29.7 6.0 %all-to-all-start = ((bf16[32,4,3,24,256]{4,3,2,1,0:T(8,128)(2,1)}), bf16[32,4,3,24,256]{4,3,2,1,0:T(8,128)(2,1)}, u32[]{:S(2)}, u32[]{:S(2)}) async-start(bf16[32,4,3,24,256]{4,3,2,1,0:T(8,128)(2,1)} %copy-done), calls=%async_computation | async-start | bytes 9437184 | tf_op jit(solution)/shard_map/all_to_all | solution.py:143
  35.7 1.6 collective-permute-start
  37.3 0.5 collective-permute-start.1
  37.8 1.2 collective-permute-start.2
  39.0 198.1 %all-to-all-done = bf16[32,4,3,24,256]{4,3,2,1,0:T(8,128)(2,1)} async-done(((bf16[32,4,3,24,256]{4,3,2,1,0:T(8,128)(2,1)}), bf16[32,4,3,24,256]{4,3,2,1,0:T(8,128)(2,1)}, u32[]{:S(2)}, u32[]{:S(2)}) %all-to-all-start) | async-done | bytes 4718624 | tf_op jit(solution)/shard_map/all_to_all | solution.py:143
  237.2 7.2 %copy.13 = bf16[8,4,4,3,24,256]{5,0,2,1,3,4:T(8,128)(2,1)} copy(bf16[8,4,4,3,24,256]{5,4,3,2,1,0:T(8,128)(2,1)} %bitcast.6) | data formatting | bytes 9437184 | tf_op jit(solution)/shard_map/reshape | solution.py:144
  244.3 41.6 %collective-permute-done.refs_1_ = bf16[23,3,64,256]{3,2,1,0:T(8,128)(2,1)S(1)} collective-permute-done((bf16[23,3,64,256]{3,2,1,0:T(8,128)(2,1)}, bf16[23,3,64,256]{3,2,1,0:T(8,128)(2,1)S(1)}, u32[]{:S(2)}, u32[]{:S(2)}) %collective-permute-start) | collective-permute-done | bytes 2261024 | tf_op jit(solution)/shard_map/ppermute | solution.py:117
  285.9 0.0 collective-permute-done.1.refs_2_
  285.9 47.7 %collective-permute-done.2.refs_3_ = bf16[23,3,64,256]{3,2,1,0:T(8,128)(2,1)} collective-permute-done((bf16[23,3,64,256]{3,2,1,0:T(8,128)(2,1)}, bf16[23,3,64,256]{3,2,1,0:T(8,128)(2,1)}, u32[]{:S(2)}, u32[]{:S(2)}) %collective-permute-start.2) | collective-permute-done | bytes 2261024 | tf_op jit(solution)/shard_map/ppermute | solution.py:117
  333.6 19.5 %mix.1 = bf16[24,3,4,32,256]{4,3,2,1,0:T(8,128)(2,1)} custom-call(s32[1]{0:T(128)} %bitcast.3.where_ref, bf16[24,3,4,32,256]{4,3,2,1,0:T(8,128)(2,1)} %bitcast.22, bf16[92,3,64,256]{3,2,1,0:T(8,128)(2,1)} %refs_0_.1, bf16[23,3,64,256]{3,2,1,0:T(8,128)(2,1)S(1)} %collective-permute-done.refs_1_, bf16[23,3,64,256]{3,2,1,0:T(8,128)(2,1)} %collective-permute-done.1.refs_2_, ...), custom_call_target="tpu_custom_call" | custom-call | tf_op jit(solution)/shard_map/mix/pallas_call | solution.py:155
  353.1 5.0 %copy.10 = bf16[24,3,4,4,8,256]{5,0,1,3,2,4:T(8,128)(2,1)S(1)} copy(bf16[24,3,4,4,8,256]{5,4,3,2,1,0:T(8,128)(2,1)} %bitcast.23) | data formatting | bytes 9437184 | tf_op jit(solution)/shard_map/reshape | solution.py:168
  358.1 108.4 %all_to_all.10.mixed_ref = bf16[32,4,3,24,256]{4,3,2,1,0:T(8,128)(2,1)S(1)} all-to-all(bf16[32,4,3,24,256]{4,3,2,1,0:T(8,128)(2,1)S(1)} %bitcast.21), channel_id=1, replica_groups=mesh['order'=8,'chan'=4] {'order','chan'}, dimensions={0} | all-to-all | bytes 9437184 | tf_op jit(solution)/shard_map/all_to_all | solution.py:170
  466.5 17.5 %synthesise.1 = bf16[4,3,256,720]{3,2,1,0:T(8,128)(2,1)} custom-call(s32[4]{0:T(128)S(1)} %copy-done.1, s32[768,1]{1,0:T(8,128)S(1)} %copy.11.degree_ref, bf16[4,3,720,721]{3,2,1,0:T(8,128)(2,1)} %bitcast.26, bf16[32,4,3,24,256]{4,3,2,1,0:T(8,128)(2,1)S(1)} %all_to_all.10.mixed_ref), custom_call_target="tpu_custom_call" | custom-call | flops 6378946560 | bytes 24917760 | tf_op jit(solution)/shard_map/synthesise/pallas_call | solution.py:172
  (2 shorter events, 0.0 us)
Async XLA Ops:
  2.4 6.2 %copy-start.1 = (s32[4]{0:T(128)S(1)}, s32[4]{0:T(128)}, u32[]{:S(2)}) copy-start(s32[4]{0:T(128)} %order_ref.3) | copy-start | bytes 52
  27.5 2.2 copy-start
  29.7 207.4 %all-to-all-start = ((bf16[32,4,3,24,256]{4,3,2,1,0:T(8,128)(2,1)}), bf16[32,4,3,24,256]{4,3,2,1,0:T(8,128)(2,1)}, u32[]{:S(2)}, u32[]{:S(2)}) async-start(bf16[32,4,3,24,256]{4,3,2,1,0:T(8,128)(2,1)} %copy-done), calls=%async_computation | async-start | bytes 9437184 | tf_op jit(solution)/shard_map/all_to_all | solution.py:143
  35.7 250.2 %collective-permute-start = (bf16[23,3,64,256]{3,2,1,0:T(8,128)(2,1)}, bf16[23,3,64,256]{3,2,1,0:T(8,128)(2,1)S(1)}, u32[]{:S(2)}, u32[]{:S(2)}) collective-permute-start(bf16[23,3,64,256]{3,2,1,0:T(8,128)(2,1)} %get-tuple-element.10), channel_id=1, source_target_pairs={{0,1},{1,2},{2,3},{3,0},{4,5},{5,6},{6,7},{7,4},{8,9},{9,10},{10,1... | collective-permute-start | bytes 6782984 | tf_op jit(solution)/shard_map/ppermute | solution.py:117
  37.3 248.6 %collective-permute-start.1 = (bf16[23,3,64,256]{3,2,1,0:T(8,128)(2,1)}, bf16[23,3,64,256]{3,2,1,0:T(8,128)(2,1)}, u32[]{:S(2)}, u32[]{:S(2)}) collective-permute-start(bf16[23,3,64,256]{3,2,1,0:T(8,128)(2,1)} %get-tuple-element.11), channel_id=1, source_target_pairs={{0,2},{1,3},{2,0},{3,1},{4,6},{5,7},{6,4},{7,5},{8,10},{9,11},{10,... | collective-permute-start | bytes 6782984 | tf_op jit(solution)/shard_map/ppermute | solution.py:117
  37.8 295.8 %collective-permute-start.2 = (bf16[23,3,64,256]{3,2,1,0:T(8,128)(2,1)}, bf16[23,3,64,256]{3,2,1,0:T(8,128)(2,1)}, u32[]{:S(2)}, u32[]{:S(2)}) collective-permute-start(bf16[23,3,64,256]{3,2,1,0:T(8,128)(2,1)} %get-tuple-element.12), channel_id=1, source_target_pairs={{0,3},{1,0},{2,1},{3,2},{4,7},{5,4},{6,5},{7,6},{8,11},{9,8},{10,9... | collective-permute-start | bytes 6782984 | tf_op jit(solution)/shard_map/ppermute | solution.py:117
